TPU v7x, 512 devices: a whole 4x8x8 slice. The times are simulated.
512 devices in a mesh: dp: 8 (over x, core), ctx: 64 (over y, z).
Axes of the slice: x: 4, y: 8, z: 8, core: 2. Of those that a mesh axis runs over, the one named last changes fastest.
Arguments:
- token_ids: int32 [8, 8192], P('dp', 'ctx'), may hold values from 0 to 7
- queries: bfloat16 [8, 8192, 4096], P('dp', 'ctx'), may hold values from -6 to 6
- gated_values: bfloat16 [8, 8192, 4096], P('dp', 'ctx'), may hold values from -6 to 6
- out_grad: bfloat16 [8, 8192, 4096], P('dp', 'ctx'), may hold values from -6 to 6
- filters: bfloat16 [4096, 128], P('ctx'), may hold values from -0.5 to 0.5
Outputs:
- value_grad: bfloat16 [8, 8192, 4096], P('dp', 'ctx')
- filter_grad: float32 [4096, 128], P('ctx')
Inputs may be any that keep to these rules, and one draw needn't show every extreme that they name: `token_ids`: ids 0 to 3 are upper-case bases, 4 to 7 lower-case bases.
All inputs are finite; a program needn't handle non-finite values.
Results may differ from a plain program's by a relative error of at most 0.0049.
Values may be sent and summed in bfloat16 or wider, within the bound.
A program may use at most 64 MiB of HBM per device.

v0:
```python
import jax
import jax.numpy as jnp
import numpy as np
from jax import lax
from jax.sharding import PartitionSpec as P


def tables(span):
    half = span // 2
    angle = np.pi * (2 * np.arange(half)[:, None] + 1) * np.arange(span)[None, :] / span
    wave = np.concatenate([np.cos(angle), np.sin(angle)], axis=0)
    high = wave.astype(jnp.bfloat16)
    low = (wave - high.astype(np.float64)).astype(jnp.bfloat16)
    return (high, low)


def mul(a, b):
    return jnp.dot(a, b, preferred_element_type=jnp.float32)


def body(token_ids, queries, gated_values, out_grad, filters):
    dp, ctx = (lax.axis_size("dp"), lax.axis_size("ctx"))
    weight = jnp.where(token_ids < 4, 1.0, 0.1).astype(jnp.float32)
    cotangent = (
        weight[:, :, None] * out_grad.astype(jnp.float32) * queries.astype(jnp.float32)
    ).astype(jnp.bfloat16)[0]
    rows = cotangent.shape[0]
    factor_tok = float(dp * ctx * rows) ** (-0.5)
    taps = lax.all_gather(filters, "ctx", axis=0, tiled=True)
    after = lax.ppermute(cotangent, "ctx", [(i, i - 1) for i in range(1, ctx)])
    high, low = (jnp.asarray(t) for t in tables(2 * rows))

    def forward(x):
        n = x.shape[0]
        wave = mul(high[:, :n], x) + mul(low[:, :n], x)
        return (wave[:rows], wave[rows:])

    def backward(re, im):
        both = jnp.concatenate([re, im], axis=0) * (1.0 / rows)
        top = both.astype(jnp.bfloat16)
        rest = (both - top.astype(jnp.float32)).astype(jnp.bfloat16)
        up, down = (high[:, :rows].T, low[:, :rows].T)
        return mul(up, top) + (mul(up, rest) + mul(down, top))

    cot_cos, cot_sin = forward(jnp.concatenate([cotangent, after], axis=0))

    def correlate(x):
        x_cos, x_sin = forward(x)
        return backward(cot_cos * x_cos + cot_sin * x_sin, cot_sin * x_cos - cot_cos * x_sin)

    tap_part = correlate(gated_values[0]).T * factor_tok
    filter_grad = lax.psum(lax.psum_scatter(tap_part, "ctx", scatter_dimension=0, tiled=True), "dp")
    value_grad = correlate(taps.T).astype(jnp.bfloat16)[None]
    return (value_grad, filter_grad)


def solution(mesh):
    return jax.shard_map(
        body,
        mesh=mesh,
        in_specs=(
            P("dp", "ctx"),
            P("dp", "ctx", None),
            P("dp", "ctx", None),
            P("dp", "ctx", None),
            P("ctx", None),
        ),
        out_specs=(P("dp", "ctx", None), P("ctx", None)),
        check_vma=False,
    )
```

profile of v0, /device:TPU:16, one launch (start us, length us, event | category | flops | bytes accessed | tf_op | source)
XLA Modules:
  0.0 386.2 jit_solution(3704554985823753769)
XLA Ops:
  7.2 0.0 copy-start
  7.2 0.0 copy-start.5
  7.2 0.0 all-gather.2.cloned.1.call-start
  7.2 0.7 all-gather.2.cloned.1.call-update
  7.9 0.0 reduce-scatter.2.cloned.1.call-start
  8.0 0.7 fusion.25
  8.6 1.9 fusion.13
  10.6 0.0 copy-start.4
  10.6 11.0 %collective-permute-start = (bf16[128,4096]{1,0:T(8,128)(2,1)S(1)}, bf16[128,4096]{1,0:T(8,128)(2,1)S(1)}, u32[]{:S(2)}, u32[]{:S(2)}) collective-permute-start(bf16[128,4096]{1,0:T(8,128)(2,1)S(1)} %fusion.13), channel_id=1, source_target_pairs={{1,0},{2,1},{3,2},{4,3},{5,4},{6,5},{7,6},{8,7},{9,8},{10,9},{11,1... | collective-permute-start | bytes 3145736 | tf_op jit(solution)/shard_map/ppermute | solution.py:30
  21.6 0.0 copy-done.5
  21.6 0.7 fusion.40
  22.3 0.0 copy-done.4
  22.3 0.7 fusion.39
  23.0 0.0 copy-done
  23.0 0.7 fusion.15
  23.7 0.0 copy-start.7
  23.7 2.7 convolution_add_fusion.2
  26.4 0.0 copy-start.6
  26.4 17.9 %collective-permute-done = bf16[128,4096]{1,0:T(8,128)(2,1)S(1)} collective-permute-done((bf16[128,4096]{1,0:T(8,128)(2,1)S(1)}, bf16[128,4096]{1,0:T(8,128)(2,1)S(1)}, u32[]{:S(2)}, u32[]{:S(2)}) %collective-permute-start) | collective-permute-done | bytes 1048608 | tf_op jit(solution)/shard_map/ppermute | solution.py:30
  44.3 0.0 copy-done.7
  44.3 0.7 convolution_add_fusion.1
  45.0 0.0 copy-done.6
  45.0 2.7 fusion.1
  47.7 49.9 %all-gather.2.cloned.1.call-done = bf16[4096,128]{1,0:T(8,128)(2,1)} async-done(((bf16[64,128]{1,0:T(8,128)(2,1)}), bf16[4096,128]{1,0:T(8,128)(2,1)}) %all-gather.2.cloned.1.call-update) | async-done | bytes 1048592 | tf_op jit(solution)/shard_map/all_gather | solution.py:29
  97.6 0.0 copy-start.3
  97.6 2.0 fusion.38
  99.6 0.0 copy-done.3
  99.6 0.0 copy-start.2
  99.6 2.7 convolution_add_fusion.3
  102.4 0.7 copy-done.2
  103.1 6.1 %multiply_add_fusion = (f32[128,4096]{1,0:T(8,128)S(1)}, f32[128,4096]{1,0:T(8,128)S(1)}, f32[128,4096]{1,0:T(8,128)S(1)}, f32[128,4096]{1,0:T(8,128)}) fusion(f32[256,4096]{1,0:T(8,128)S(1)} %copy-done.2, f32[256,4096]{1,0:T(8,128)} %fusion.1, f32[256,4096]{1,0:T(8,128)} %convolution_add_fusion.3), kind=kLoop, calls=%fused_computation.22 | loop fusion | flops 6291456 | bytes 20971520 | tf_op jit(solution)/shard_map/add | solution.py:49
  109.2 0.8 fusion.10
  110.0 0.8 fusion.23
  110.7 2.1 fusion.3
  112.8 0.0 reduce-scatter.2.cloned.1.call-update
  112.9 0.0 copy-start.1
  112.9 2.5 fusion.9
  115.4 0.0 copy-done.1
  115.4 0.8 fusion.19
  116.2 1.9 fusion.6
  118.1 2.3 copy.9
  120.4 234.3 %reduce-scatter.2.cloned.1.call-done = f32[64,128]{1,0:T(8,128)} async-done(((f32[4096,128]{1,0:T(8,128)}), f32[64,128]{1,0:T(8,128)}) %reduce-scatter.2.cloned.1.call-update) | async-done | bytes 32784 | tf_op jit(solution)/shard_map/reduce_scatter | solution.py:52
  354.7 24.7 %psum.7 = f32[64,128]{1,0:T(8,128)} all-reduce(f32[64,128]{1,0:T(8,128)} %reduce-scatter.2.cloned.1.call-done), channel_id=1, replica_groups=mesh['dp'=8,'ctx'=64] {'dp'}, use_global_device_ids=true, to_apply=%region_1.2 | all-reduce | flops 8192 | bytes 65536 | tf_op jit(solution)/shard_map/psum | solution.py:52
Async XLA Ops:
  7.2 15.8 %copy-start = (bf16[1,128,4096]{2,1,0:T(8,128)(2,1)S(1)}, bf16[1,128,4096]{2,1,0:T(8,128)(2,1)}, u32[]{:S(2)}) copy-start(bf16[1,128,4096]{2,1,0:T(8,128)(2,1)} %param.9) | copy-start | bytes 3145732
  7.2 14.4 %copy-start.5 = (bf16[256,128]{1,0:T(8,128)(2,1)S(1)}, bf16[256,128]{1,0:T(8,128)(2,1)}, u32[]{:S(2)}) copy-start(bf16[256,128]{1,0:T(8,128)(2,1)} %constant.22) | copy-start | bytes 196612
  7.2 90.4 %all-gather.2.cloned.1.call-start = ((), (), s32[]{:S(2)}) async-start(), calls=%async_computation.1 | async-start | bytes 1064960 | tf_op jit(solution)/shard_map/all_gather | solution.py:29
  7.9 346.8 %reduce-scatter.2.cloned.1.call-start = ((), (), s32[]{:S(2)}) async-start(), calls=%async_computation.2 | async-start | bytes 2129920 | tf_op jit(solution)/shard_map/reduce_scatter | solution.py:52
  10.6 11.7 %copy-start.4 = (bf16[256,128]{1,0:T(8,128)(2,1)S(1)}, bf16[256,128]{1,0:T(8,128)(2,1)}, u32[]{:S(2)}) copy-start(bf16[256,128]{1,0:T(8,128)(2,1)} %constant.20) | copy-start | bytes 196612
  10.6 33.7 %collective-permute-start = (bf16[128,4096]{1,0:T(8,128)(2,1)S(1)}, bf16[128,4096]{1,0:T(8,128)(2,1)S(1)}, u32[]{:S(2)}, u32[]{:S(2)}) collective-permute-start(bf16[128,4096]{1,0:T(8,128)(2,1)S(1)} %fusion.13), channel_id=1, source_target_pairs={{1,0},{2,1},{3,2},{4,3},{5,4},{6,5},{7,6},{8,7},{9,8},{10,9},{11,1... | collective-permute-start | bytes 3145736 | tf_op jit(solution)/shard_map/ppermute | solution.py:30
  23.7 20.6 %copy-start.7 = (bf16[256,128]{1,0:T(8,128)(2,1)S(1)}, bf16[256,128]{1,0:T(8,128)(2,1)}, u32[]{:S(2)}) copy-start(bf16[256,128]{1,0:T(8,128)(2,1)} %constant.21) | copy-start | bytes 196612
  26.4 18.6 %copy-start.6 = (bf16[256,128]{1,0:T(8,128)(2,1)S(1)}, bf16[256,128]{1,0:T(8,128)(2,1)}, u32[]{:S(2)}) copy-start(bf16[256,128]{1,0:T(8,128)(2,1)} %constant.23) | copy-start | bytes 196612
  97.6 2.0 copy-start.3
  99.6 3.5 copy-start.2
  112.9 2.5 copy-start.1
Sparse Core Ops, SparseCore 0:
  11.0 86.4 all-gather.1
  113.0 241.6 reduce-scatter.1
where the time goes:
time: 387 us; the launch traced here: 386 us
  waiting for transfers between devices  303 us (78%)
  blocking collectives  24.7 us (6%)
  matrix products  21.8 us (6%)
  between operations  14.2 us (4%)
  starting transfers between devices  11 us (3%)
  other arithmetic  8.73 us (2%)
    reduce_scatter x1, waiting for transfers between devices, body(): lax.psum_scatter(tap_part, 'ctx', scatter_dimension=0, tiled=True)  234 us
    all_gather x1, waiting for transfers between devices, body(): taps = lax.all_gather(filters, 'ctx', axis=0, tiled=True)  49.9 us
    psum x1, blocking collectives, body(): lax.psum(lax.psum_scatter(tap_part, 'ctx', scatter_dimension=0, tiled=Tru...  24.7 us
    dot_general x14, matrix products, mul(): return jnp.dot(a, b, preferred_element_type=jnp.float32)  21.8 us
    ppermute x1, waiting for transfers between devices, body(): after = lax.ppermute(cotangent, 'ctx', [(i, i - 1) for i in range(1, ctx)])  17.9 us
    ppermute x1, starting transfers between devices, body(): after = lax.ppermute(cotangent, 'ctx', [(i, i - 1) for i in range(1, ctx)])  11 us
  transfers between devices with their start and end apart: 3, of which 3 were waited for; matrix products, arithmetic and copies ran while one was open for 5% of the time, Pallas kernels for 0%

commit v1 on v0

--- a/solution.py
+++ b/solution.py
@@ -26,7 +26,15 @@
     ).astype(jnp.bfloat16)[0]
     rows = cotangent.shape[0]
     factor_tok = float(dp * ctx * rows) ** (-0.5)
-    taps = lax.all_gather(filters, "ctx", axis=0, tiled=True)
+    ways, here = (lax.axis_size("ctx"), lax.axis_index("ctx"))
+    grown, reach = (filters, 1)
+    while reach < ways:
+        theirs = lax.ppermute(grown, "ctx", [(d, d ^ reach) for d in range(ways)])
+        mine_first = jnp.concatenate([grown, theirs], axis=0)
+        theirs_first = jnp.concatenate([theirs, grown], axis=0)
+        grown = jnp.where(here & reach == 0, mine_first, theirs_first)
+        reach = 2 * reach
+    taps = grown
     after = lax.ppermute(cotangent, "ctx", [(i, i - 1) for i in range(1, ctx)])
     high, low = (jnp.asarray(t) for t in tables(2 * rows))
 

time: 387 us -> 395 us (1.021)
  starting transfers between devices: 11 us -> 35 us
  waiting for transfers between devices: 303 us -> 279 us
  matrix products: 21.8 us -> 29.4 us
    all_gather x1 -> x0, waiting for transfers between devices: 49.9 us -> none  [body(): taps = lax.all_gather(filters, 'ctx', axis=0, tiled=True)]
    ppermute x0 -> x6, waiting for transfers between devices: none -> 39.4 us  [body(): theirs = lax.ppermute(grown, 'ctx', [(d, d ^ reach) for d in range(ways)])]
    ppermute x0 -> x6, starting transfers between devices: none -> 32.8 us  [body(): theirs = lax.ppermute(grown, 'ctx', [(d, d ^ reach) for d in range(ways)])]
    ppermute x1, waiting for transfers between devices: 17.9 us -> 0.01 us  [body(): after = lax.ppermute(cotangent, 'ctx', [(i, i - 1) for i in range(1, ctx)])]
    ppermute x1, starting transfers between devices: 11 us -> 2.18 us  [body(): after = lax.ppermute(cotangent, 'ctx', [(i, i - 1) for i in range(1, ctx)])]
    dot_general x14, matrix products: 21.8 us -> 29.4 us  [mul(): return jnp.dot(a, b, preferred_element_type=jnp.float32)]
    reduce_scatter x1, waiting for transfers between devices: 234 us -> 239 us  [body(): lax.psum_scatter(tap_part, 'ctx', scatter_dimension=0, tiled=True)]
  transfers between devices with their start and end apart: 3 -> 8, of which waited for: 3 -> 6; matrix products, arithmetic and copies ran while one was open for 5% -> 6% of each run, Pallas kernels for 0% -> 0%
where the time goes in v1:
time: 395 us
  waiting for transfers between devices  279 us (71%)
  starting transfers between devices  35 us (9%)
  matrix products  29.4 us (7%)
  blocking collectives  24.7 us (6%)
  between operations  14.2 us (4%)
  other arithmetic  9.84 us (2%)
    reduce_scatter x1, waiting for transfers between devices, body(): lax.psum_scatter(tap_part, 'ctx', scatter_dimension=0, tiled=True)  239 us
    ppermute x6, waiting for transfers between devices, body(): theirs = lax.ppermute(grown, 'ctx', [(d, d ^ reach) for d in range(ways)])  39.4 us
    ppermute x6, starting transfers between devices, body(): theirs = lax.ppermute(grown, 'ctx', [(d, d ^ reach) for d in range(ways)])  32.8 us
    dot_general x14, matrix products, mul(): return jnp.dot(a, b, preferred_element_type=jnp.float32)  29.4 us
    psum x1, blocking collectives, body(): lax.psum(lax.psum_scatter(tap_part, 'ctx', scatter_dimension=0, tiled=Tru...  24.7 us
  transfers between devices with their start and end apart: 8, of which 6 were waited for; matrix products, arithmetic and copies ran while one was open for 6% of the time, Pallas kernels for 0%

profile of v1, /device:TPU:16, one launch (start us, length us, event | category | flops | bytes accessed | tf_op | source)
XLA Modules:
  0.0 394.7 jit_solution(1865737707075941602)
XLA Ops:
  7.2 0.0 copy-start
  7.2 0.0 copy-start.4
  7.2 0.0 reduce-scatter.2.cloned.1.call-start
  7.2 4.4 %collective-permute-start.1 = (bf16[64,128]{1,0:T(8,128)(2,1)}, bf16[64,128]{1,0:T(8,128)(2,1)S(1)}, u32[]{:S(2)}, u32[]{:S(2)}) collective-permute-start(bf16[64,128]{1,0:T(8,128)(2,1)} %param.11), channel_id=1, source_target_pairs={{0,1},{1,0},{2,3},{3,2},{4,5},{5,4},{6,7},{7,6},{8,9},{9,8},{10,11... | collective-permute-start | bytes 49160 | tf_op jit(solution)/shard_map/ppermute | solution.py:32
  11.7 1.9 collective-permute-done.1
  13.6 0.8 maximum_select_fusion.7
  14.4 6.1 %collective-permute-start.2 = (bf16[128,128]{1,0:T(8,128)(2,1)S(1)}, bf16[128,128]{1,0:T(8,128)(2,1)S(1)}, u32[]{:S(2)}, u32[]{:S(2)}) collective-permute-start(bf16[128,128]{1,0:T(8,128)(2,1)S(1)} %maximum_select_fusion.7), channel_id=1, source_target_pairs={{0,2},{1,3},{2,0},{3,1},{4,6},{5,7},{6,4},{7,5},{8,10},{9,11},{10,... | collective-permute-start | bytes 98312 | tf_op jit(solution)/shard_map/ppermute | solution.py:32
  20.5 0.7 fusion.27
  21.1 1.2 collective-permute-done.2
  22.4 9.3 %collective-permute-start.3 = (bf16[256,128]{1,0:T(8,128)(2,1)S(1)}, bf16[256,128]{1,0:T(8,128)(2,1)S(1)}, u32[]{:S(2)}, u32[]{:S(2)}) collective-permute-start(bf16[256,128]{1,0:T(8,128)(2,1)S(1)} %maximum_select_fusion.6), channel_id=1, source_target_pairs={{0,4},{1,5},{2,6},{3,7},{4,0},{5,1},{6,2},{7,3},{8,12},{9,13},{10,... | collective-permute-start | bytes 196616 | tf_op jit(solution)/shard_map/ppermute | solution.py:32
  31.7 1.9 fusion.14
  33.6 2.2 collective-permute-start
  35.8 0.0 collective-permute-done.3
  35.9 0.0 copy-start.5
  35.9 3.6 collective-permute-start.4
  39.5 0.0 copy-done
  39.5 0.0 copy-done.4
  39.5 2.7 fusion.16
  42.2 19.6 %collective-permute-done.4 = bf16[512,128]{1,0:T(8,128)(2,1)S(1)} collective-permute-done((bf16[512,128]{1,0:T(8,128)(2,1)S(1)}, bf16[512,128]{1,0:T(8,128)(2,1)S(1)}, u32[]{:S(2)}, u32[]{:S(2)}) %collective-permute-start.4) | collective-permute-done | bytes 131104 | tf_op jit(solution)/shard_map/ppermute | solution.py:32
  61.8 0.1 maximum_select_fusion.2
  61.9 1.9 collective-permute-start.5
  63.8 0.0 copy-done.5
  63.8 4.9 %convolution_add_fusion.2 = f32[256,4096]{1,0:T(8,128)} fusion(f32[256,4096]{1,0:T(8,128)} %fusion.16, bf16[256,128]{1,0:T(8,128)(2,1)S(1)} %copy-done.5, bf16[1,128,4096]{2,1,0:T(8,128)(2,1)S(1)} %copy-done), kind=kOutput, calls=%fused_computation.4 | convolution fusion | flops 269484032 | bytes 9502720 | tf_op jit(solution)/shard_map/dot_general | solution.py:18
  68.7 2.9 collective-permute-done.5
  71.6 0.1 maximum_select_fusion.1
  71.8 7.5 %collective-permute-start.6 = (bf16[2048,128]{1,0:T(8,128)(2,1)S(1)}, bf16[2048,128]{1,0:T(8,128)(2,1)S(1)}, u32[]{:S(2)}, u32[]{:S(2)}) collective-permute-start(bf16[2048,128]{1,0:T(8,128)(2,1)S(1)} %maximum_select_fusion.1), channel_id=1, source_target_pairs={{0,32},{1,33},{2,34},{3,35},{4,36},{5,37},{6,38},{7,39},{8,40},{9,... | collective-permute-start | bytes 1572872 | tf_op jit(solution)/shard_map/ppermute | solution.py:32
  79.2 2.7 fusion.43
  81.9 0.7 fusion.42
  82.6 13.8 %collective-permute-done.6 = bf16[2048,128]{1,0:T(8,128)(2,1)S(1)} collective-permute-done((bf16[2048,128]{1,0:T(8,128)(2,1)S(1)}, bf16[2048,128]{1,0:T(8,128)(2,1)S(1)}, u32[]{:S(2)}, u32[]{:S(2)}) %collective-permute-start.6) | collective-permute-done | bytes 524320 | tf_op jit(solution)/shard_map/ppermute | solution.py:32
  96.4 0.7 fusion.18
  97.1 0.0 copy-start.7
  97.1 2.7 fusion.2
  99.8 0.0 copy-start.6
  99.8 0.0 collective-permute-done
  99.8 0.0 copy-done.7
  99.8 0.0 copy-start.3
  99.8 2.1 convolution_add_fusion.1
  101.9 0.0 copy-done.6
  101.9 0.4 copy-done.3
  102.4 0.0 copy-start.2
  102.4 4.1 %fusion.1 = f32[256,4096]{1,0:T(8,128)} fusion(f32[4096,256]{0,1:T(8,128)S(1)} %convolution_add_fusion.1, f32[4096,256]{0,1:T(8,128)S(1)} %copy-done.3, bf16[256,128]{1,0:T(8,128)(2,1)S(1)} %copy-done.6, bf16[128,4096]{1,0:T(8,128)(2,1)} %collective-permute-done), kind=kOutput, calls=%fused_computation.2 | convolution fusion | flops 270532608 | bytes 13697024 | tf_op jit(solution)/shard_map/dot_general | solution.py:18
  106.5 0.0 copy-done.2
  106.5 6.2 %multiply_add_fusion = (f32[128,4096]{1,0:T(8,128)S(1)}, f32[128,4096]{1,0:T(8,128)S(1)}, f32[128,4096]{1,0:T(8,128)S(1)}, f32[128,4096]{1,0:T(8,128)}) fusion(f32[256,4096]{1,0:T(8,128)S(1)} %copy-done.2, f32[256,4096]{1,0:T(8,128)} %fusion.1, f32[256,4096]{1,0:T(8,128)} %fusion.2), kind=kLoop, calls=%fused_computation.23 | loop fusion | flops 6291456 | bytes 20971520 | tf_op jit(solution)/shard_map/add | solution.py:57
  112.7 0.8 fusion.11
  113.4 0.8 fusion.25
  114.2 2.1 fusion.4
  116.3 0.0 reduce-scatter.2.cloned.1.call-update
  116.3 0.0 copy-start.1
  116.3 2.5 fusion.10
  118.8 0.0 copy-done.1
  118.8 0.8 fusion.21
  119.7 1.9 fusion.7
  121.6 2.3 copy.9
  123.8 239.3 %reduce-scatter.2.cloned.1.call-done = f32[64,128]{1,0:T(8,128)} async-done(((f32[4096,128]{1,0:T(8,128)}), f32[64,128]{1,0:T(8,128)}) %reduce-scatter.2.cloned.1.call-update) | async-done | bytes 32784 | tf_op jit(solution)/shard_map/reduce_scatter | solution.py:60
  363.1 24.7 %psum.7 = f32[64,128]{1,0:T(8,128)} all-reduce(f32[64,128]{1,0:T(8,128)} %reduce-scatter.2.cloned.1.call-done), channel_id=1, replica_groups=mesh['dp'=8,'ctx'=64] {'dp'}, use_global_device_ids=true, to_apply=%region_1.2 | all-reduce | flops 8192 | bytes 65536 | tf_op jit(solution)/shard_map/psum | solution.py:60
  (2 shorter events, 0.1 us)
Async XLA Ops:
  7.2 32.3 %copy-start = (bf16[1,128,4096]{2,1,0:T(8,128)(2,1)S(1)}, bf16[1,128,4096]{2,1,0:T(8,128)(2,1)}, u32[]{:S(2)}) copy-start(bf16[1,128,4096]{2,1,0:T(8,128)(2,1)} %param.9) | copy-start | bytes 3145732
  7.2 32.3 %copy-start.4 = (bf16[256,128]{1,0:T(8,128)(2,1)S(1)}, bf16[256,128]{1,0:T(8,128)(2,1)}, u32[]{:S(2)}) copy-start(bf16[256,128]{1,0:T(8,128)(2,1)} %constant.37) | copy-start | bytes 196612
  7.2 355.9 %reduce-scatter.2.cloned.1.call-start = ((), (), s32[]{:S(2)}) async-start(), calls=%async_computation.1 | async-start | bytes 2129920 | tf_op jit(solution)/shard_map/reduce_scatter | solution.py:60
  7.2 6.3 %collective-permute-start.1 = (bf16[64,128]{1,0:T(8,128)(2,1)}, bf16[64,128]{1,0:T(8,128)(2,1)S(1)}, u32[]{:S(2)}, u32[]{:S(2)}) collective-permute-start(bf16[64,128]{1,0:T(8,128)(2,1)} %param.11), channel_id=1, source_target_pairs={{0,1},{1,0},{2,3},{3,2},{4,5},{5,4},{6,7},{7,6},{8,9},{9,8},{10,11... | collective-permute-start | bytes 49160 | tf_op jit(solution)/shard_map/ppermute | solution.py:32
  14.4 8.0 %collective-permute-start.2 = (bf16[128,128]{1,0:T(8,128)(2,1)S(1)}, bf16[128,128]{1,0:T(8,128)(2,1)S(1)}, u32[]{:S(2)}, u32[]{:S(2)}) collective-permute-start(bf16[128,128]{1,0:T(8,128)(2,1)S(1)} %maximum_select_fusion.7), channel_id=1, source_target_pairs={{0,2},{1,3},{2,0},{3,1},{4,6},{5,7},{6,4},{7,5},{8,10},{9,11},{10,... | collective-permute-start | bytes 98312 | tf_op jit(solution)/shard_map/ppermute | solution.py:32
  22.4 13.4 %collective-permute-start.3 = (bf16[256,128]{1,0:T(8,128)(2,1)S(1)}, bf16[256,128]{1,0:T(8,128)(2,1)S(1)}, u32[]{:S(2)}, u32[]{:S(2)}) collective-permute-start(bf16[256,128]{1,0:T(8,128)(2,1)S(1)} %maximum_select_fusion.6), channel_id=1, source_target_pairs={{0,4},{1,5},{2,6},{3,7},{4,0},{5,1},{6,2},{7,3},{8,12},{9,13},{10,... | collective-permute-start | bytes 196616 | tf_op jit(solution)/shard_map/ppermute | solution.py:32
  33.6 66.2 %collective-permute-start = (bf16[128,4096]{1,0:T(8,128)(2,1)S(1)}, bf16[128,4096]{1,0:T(8,128)(2,1)}, u32[]{:S(2)}, u32[]{:S(2)}) collective-permute-start(bf16[128,4096]{1,0:T(8,128)(2,1)S(1)} %fusion.14), channel_id=1, source_target_pairs={{1,0},{2,1},{3,2},{4,3},{5,4},{6,5},{7,6},{8,7},{9,8},{10,9},{11,1... | collective-permute-start | bytes 3145736 | tf_op jit(solution)/shard_map/ppermute | solution.py:38
  35.9 28.0 %copy-start.5 = (bf16[256,128]{1,0:T(8,128)(2,1)S(1)}, bf16[256,128]{1,0:T(8,128)(2,1)}, u32[]{:S(2)}) copy-start(bf16[256,128]{1,0:T(8,128)(2,1)} %constant.39) | copy-start | bytes 196612
  35.9 25.9 %collective-permute-start.4 = (bf16[512,128]{1,0:T(8,128)(2,1)S(1)}, bf16[512,128]{1,0:T(8,128)(2,1)S(1)}, u32[]{:S(2)}, u32[]{:S(2)}) collective-permute-start(bf16[512,128]{1,0:T(8,128)(2,1)S(1)} %maximum_select_fusion.5), channel_id=1, source_target_pairs={{0,8},{1,9},{2,10},{3,11},{4,12},{5,13},{6,14},{7,15},{8,0},{9,1},... | collective-permute-start | bytes 393224 | tf_op jit(solution)/shard_map/ppermute | solution.py:32
  61.9 9.7 %collective-permute-start.5 = (bf16[1024,128]{1,0:T(8,128)(2,1)S(1)}, bf16[1024,128]{1,0:T(8,128)(2,1)S(1)}, u32[]{:S(2)}, u32[]{:S(2)}) collective-permute-start(bf16[1024,128]{1,0:T(8,128)(2,1)S(1)} %maximum_select_fusion.2), channel_id=1, source_target_pairs={{0,16},{1,17},{2,18},{3,19},{4,20},{5,21},{6,22},{7,23},{8,24},{9,... | collective-permute-start | bytes 786440 | tf_op jit(solution)/shard_map/ppermute | solution.py:32
  71.8 24.6 %collective-permute-start.6 = (bf16[2048,128]{1,0:T(8,128)(2,1)S(1)}, bf16[2048,128]{1,0:T(8,128)(2,1)S(1)}, u32[]{:S(2)}, u32[]{:S(2)}) collective-permute-start(bf16[2048,128]{1,0:T(8,128)(2,1)S(1)} %maximum_select_fusion.1), channel_id=1, source_target_pairs={{0,32},{1,33},{2,34},{3,35},{4,36},{5,37},{6,38},{7,39},{8,40},{9,... | collective-permute-start | bytes 1572872 | tf_op jit(solution)/shard_map/ppermute | solution.py:32
  97.1 2.7 copy-start.7
  99.8 2.1 copy-start.6
  99.8 2.5 copy-start.3
  102.4 4.2 %copy-start.2 = (f32[256,4096]{1,0:T(8,128)S(1)}, f32[256,4096]{1,0:T(8,128)}, u32[]{:S(2)}) copy-start(f32[256,4096]{1,0:T(8,128)} %convolution_add_fusion.2) | copy-start | bytes 12582916
  116.3 2.5 copy-start.1
Sparse Core Ops, SparseCore 0:
  116.4 246.6 reduce-scatter.1
